TPU v7x, 32 devices: a whole 2x2x4 slice. The times are simulated.
32 devices in a mesh: seq: 16 (over z, x, core), grp: 2 (over y).
Axes of the slice: x: 2, y: 2, z: 4, core: 2. Of those that a mesh axis runs over, the one named last changes fastest.
Arguments:
- tokens: bfloat16 [2, 8192, 768], P('grp', 'seq'), may hold values from -6 to 6
- w_qkv: bfloat16 [768, 2304], replicated, may hold values from -0.21875 to 0.21875
- w_out: bfloat16 [768, 768], replicated, may hold values from -2.5 to 2.5
- w_in: bfloat16 [768, 3072], replicated, may hold values from -0.21875 to 0.21875
- w_back: bfloat16 [3072, 768], replicated, may hold values from -0.109375 to 0.109375
- ln1_gain: float32 [768], replicated, may hold values from 0.25 to 1.75
- ln1_bias: float32 [768], replicated, may hold values from -3 to 3
- ln2_gain: float32 [768], replicated, may hold values from 0.25 to 1.75
- ln2_bias: float32 [768], replicated, may hold values from -3 to 3
- doc_units: int32 [2, 4], P('grp'), may hold values from 1 to 8, as said below
- tail_pad: int32 [2, 4], P('grp'), may hold values from 0 to 63
- global_ids: int32 [2, 4, 2], P('grp'), may hold values from 0 to 63, as said below
- rand_blocks: int32 [2, 128, 3], P('grp', 'seq'), may hold values from 0 to 127, as said below
- out_grad: bfloat16 [2, 8192, 768], P('grp', 'seq'), may hold values from -6 to 6
Outputs:
- output: bfloat16 [2, 8192, 768], P('grp', 'seq')
- tokens_grad: bfloat16 [2, 8192, 768], P('grp', 'seq')
- qkv_grad: float32 [768, 2304], P('seq')
- out_proj_grad: float32 [768, 768], P('seq')
- in_grad: float32 [768, 3072], P('seq')
- back_grad: float32 [3072, 768], P('seq')
- ln1_gain_grad: float32 [768], P('seq')
- ln1_bias_grad: float32 [768], P('seq')
- ln2_gain_grad: float32 [768], P('seq')
- ln2_bias_grad: float32 [768], P('seq')
Inputs may be any that keep to these rules, and one draw needn't show every extreme that they name: `doc_units`: per group the lengths sum to 16; the sequences lie end to end from the group's first block. `tail_pad`: padding tokens of a sequence, all in its last block. `global_ids`: each offset is less than its sequence's number of blocks. `rand_blocks`: entry [g, b, r] is a block of group g in the same sequence as block b.
All inputs are finite; a program needn't handle non-finite values.
Results may differ from a plain program's by a relative error of at most 0.013.
Values may be sent and summed in bfloat16 or wider, within the bound.
No kernel may reach another device: no remote copies, remote signals or barrier semaphores. Data moves between devices by JAX's collectives and lax.ppermute only.
A program may use at most 640 MiB of HBM per device.

v0:
```python
import jax
import jax.numpy as jnp
from jax import lax
from jax.sharding import PartitionSpec as P

HD = 64
BLK = 64
UNITB = 8
MOSTU = 8


ln_eps = 1e-12


def shifted(block, axis, distance):
    devices = range(lax.axis_size(axis))
    route = [(i - distance, i) for i in devices if i - distance in devices]
    return lax.ppermute(block, axis, route)


def norm_stats(values):
    center = values - jnp.mean(values, -1, keepdims=True)
    inv_std = lax.rsqrt(jnp.mean(center * center, -1, keepdims=True) + ln_eps)
    return (center * inv_std, inv_std)


def norm_back(grad_out, normed, inv_std, gain):
    gain_grad = jnp.sum(grad_out * normed, 0)
    bias_grad = jnp.sum(grad_out, 0)
    grad_hat = grad_out * gain
    centered = (
        grad_hat
        - jnp.mean(grad_hat, -1, keepdims=True)
        - normed * jnp.mean(grad_hat * normed, -1, keepdims=True)
    )
    return (inv_std * centered, gain_grad, bias_grad)


def gelu_exact(values):
    return jax.nn.gelu(values, approximate=False)


def block_plan(doc_len, tail_len, global_rel, rand_rows, total_blocks, first_row):
    per_dev = rand_rows.shape[0]
    doc_end = jnp.cumsum(doc_len) * UNITB
    starts = doc_end - doc_len * UNITB
    blocks = jnp.arange(total_blocks, dtype=jnp.int32)
    member = ((blocks[:, None] >= starts[None, :]) & (blocks[:, None] < doc_end[None, :])).astype(
        jnp.int32
    )

    def per_block(column):
        return jnp.sum(member * column[None, :], 1)

    seq_begin = per_block(starts)
    finish = per_block(doc_end)
    padding = per_block(tail_len)
    glob_one = per_block(global_rel[:, 0])
    glob_two = per_block(global_rel[:, 1])
    filled = jnp.where(blocks == finish - 1, BLK - padding, BLK)
    query_ids = first_row + jnp.arange(per_dev, dtype=jnp.int32)

    def own_rows(values):
        return lax.dynamic_slice_in_dim(values, first_row, per_dev)

    q_begin = own_rows(seq_begin)
    q_finish = own_rows(finish)
    before = jnp.where(query_ids - 1 >= q_begin, query_ids - 1, -1)
    follow = jnp.where(query_ids + 1 < q_finish, query_ids + 1, -1)
    fixed_part = jnp.stack(
        [before, query_ids, follow, q_begin + own_rows(glob_one), q_begin + own_rows(glob_two)], 1
    )
    candidates = jnp.concatenate([fixed_part, rand_rows], 1)
    cand_count = candidates.shape[1]
    equal_ids = candidates[:, :, None] == candidates[:, None, :]
    earlier = jnp.arange(cand_count)[:, None] > jnp.arange(cand_count)[None, :]
    repeat = jnp.any(equal_ids & earlier[None], 2)
    usable = (candidates >= 0) & jnp.logical_not(repeat)
    chosen = jnp.where(usable, candidates, query_ids[:, None])
    key_live = (jnp.arange(BLK)[None, None, :] < filled[chosen][:, :, None]) & usable[:, :, None]
    return (chosen, key_live)


def body(
    tokens,
    w_qkv,
    w_out,
    w_in,
    w_back,
    ln1_gain,
    ln1_bias,
    ln2_gain,
    ln2_bias,
    doc_units,
    tail_pad,
    global_ids,
    rand_blocks,
    out_grad,
):
    tok_rows = tokens.shape[1]
    model_width = tokens.shape[2]
    head_count = model_width // HD
    per_dev = tok_rows // BLK
    reach_devs = (per_dev + MOSTU * UNITB - 2) // per_dev
    span_devs = 2 * reach_devs + 1
    shards = lax.axis_size("seq")
    first_row = lax.axis_index("seq") * per_dev
    chosen, key_live = block_plan(
        doc_units[0], tail_pad[0], global_ids[0], rand_blocks[0], per_dev * shards, first_row
    )
    window_ids = chosen - first_row + reach_devs * per_dev
    cand_count = chosen.shape[1]
    score_scale = HD ** (-0.5)
    lap_blocks = min(per_dev, max(1, 512 // BLK))
    laps_count = per_dev // lap_blocks
    tok_f32 = tokens[0].astype(jnp.float32)
    normed_one, inv_one = norm_stats(tok_f32)
    input_one = (normed_one * ln1_gain + ln1_bias).astype(jnp.bfloat16)
    projected = jnp.dot(input_one, w_qkv, preferred_element_type=jnp.float32)
    query_rows = projected[:, :model_width].astype(jnp.bfloat16)
    keyval = projected[:, model_width:].astype(jnp.bfloat16)
    pieces = []
    for offset in range(-reach_devs, reach_devs + 1):
        pieces.append(keyval if offset == 0 else shifted(keyval, "seq", -offset))
    window = jnp.stack(pieces).reshape(span_devs * per_dev, BLK, 2, head_count, HD)
    query_laps = query_rows.reshape(laps_count, lap_blocks, BLK, head_count, HD)
    id_laps = window_ids.reshape(laps_count, lap_blocks, cand_count)
    live_laps = key_live.reshape(laps_count, lap_blocks, cand_count * BLK)

    def lap_keys(ids):
        gathered = window[ids]
        key_rows = gathered[:, :, :, 0].reshape(lap_blocks, cand_count * BLK, head_count, HD)
        val_rows = gathered[:, :, :, 1].reshape(lap_blocks, cand_count * BLK, head_count, HD)
        return (key_rows, val_rows)

    def lap_scores(query_blk, key_rows, live):
        raw_dots = jnp.einsum(
            "bqhd,bkhd->bhqk", query_blk, key_rows, preferred_element_type=jnp.float32
        )
        return jnp.where(live[:, None, None, :], raw_dots * score_scale, -1e30)

    def forward_lap(inputs):
        query_blk, ids, live = inputs
        key_rows, val_rows = lap_keys(ids)
        scores = lap_scores(query_blk, key_rows, live)
        row_max = jnp.max(scores, -1, keepdims=True)
        expo_scores = jnp.exp(scores - row_max)
        row_total = jnp.sum(expo_scores, -1, keepdims=True)
        probs_low = (expo_scores / row_total).astype(jnp.bfloat16)
        lap_context = jnp.einsum(
            "bhqk,bkhd->bqhd", probs_low, val_rows, preferred_element_type=jnp.float32
        )
        return (lap_context.astype(jnp.bfloat16), row_max + jnp.log(row_total))

    context_laps, lse_laps = lax.map(forward_lap, (query_laps, id_laps, live_laps))
    context = context_laps.reshape(tok_rows, model_width)
    hidden = tok_f32 + jnp.dot(context, w_out, preferred_element_type=jnp.float32)
    normed_two, inv_two = norm_stats(hidden)
    input_two = (normed_two * ln2_gain + ln2_bias).astype(jnp.bfloat16)
    pre_act = jnp.dot(input_two, w_in, preferred_element_type=jnp.float32)
    activ = gelu_exact(pre_act).astype(jnp.bfloat16)
    output = (hidden + jnp.dot(activ, w_back, preferred_element_type=jnp.float32)).astype(
        jnp.bfloat16
    )
    grad_out = out_grad[0]
    back_part = jnp.einsum("tf,td->fd", activ, grad_out, preferred_element_type=jnp.float32)
    d_act = jnp.dot(grad_out, w_back.T, preferred_element_type=jnp.float32)
    gelu_out, gelu_pull = jax.vjp(gelu_exact, pre_act)
    d_pre = gelu_pull(d_act)[0].astype(jnp.bfloat16)
    in_part = jnp.einsum("td,tf->df", input_two, d_pre, preferred_element_type=jnp.float32)
    d_norm2 = jnp.dot(d_pre, w_in.T, preferred_element_type=jnp.float32)
    d_second, gain_two_part, bias_two_part = norm_back(d_norm2, normed_two, inv_two, ln2_gain)
    d_hidden = grad_out.astype(jnp.float32) + d_second
    d_hidden_low = d_hidden.astype(jnp.bfloat16)
    out_part = jnp.einsum("te,td->ed", context, d_hidden_low, preferred_element_type=jnp.float32)
    d_context = jnp.dot(d_hidden_low, w_out.T, preferred_element_type=jnp.float32).astype(
        jnp.bfloat16
    )
    d_context_laps = d_context.reshape(laps_count, lap_blocks, BLK, head_count, HD)

    def backward_lap(grad_window, inputs):
        query_blk, ids, live, log_total, d_ctx = inputs
        key_rows, val_rows = lap_keys(ids)
        scores = lap_scores(query_blk, key_rows, live)
        probs_f32 = jnp.exp(scores - log_total)
        probs_low = probs_f32.astype(jnp.bfloat16)
        d_probs = jnp.einsum("bqhd,bkhd->bhqk", d_ctx, val_rows, preferred_element_type=jnp.float32)
        d_vals = jnp.einsum("bhqk,bqhd->bkhd", probs_low, d_ctx, preferred_element_type=jnp.float32)
        delta = jnp.sum(d_probs * probs_f32, -1, keepdims=True)
        d_scores = (probs_f32 * (d_probs - delta) * score_scale).astype(jnp.bfloat16)
        lap_dquery = jnp.einsum(
            "bhqk,bkhd->bqhd", d_scores, key_rows, preferred_element_type=jnp.float32
        )
        d_keys = jnp.einsum(
            "bhqk,bqhd->bkhd", d_scores, query_blk, preferred_element_type=jnp.float32
        )
        d_gathered = jnp.stack(
            [
                d_keys.reshape(lap_blocks * cand_count, BLK, head_count, HD),
                d_vals.reshape(lap_blocks * cand_count, BLK, head_count, HD),
            ],
            2,
        )
        grad_window = grad_window.at[ids.reshape(lap_blocks * cand_count)].add(d_gathered)
        return (grad_window, lap_dquery.astype(jnp.bfloat16))

    empty_window = jnp.zeros((span_devs * per_dev, BLK, 2, head_count, HD), jnp.float32)
    grad_window, dquery_laps = lax.scan(
        backward_lap, empty_window, (query_laps, id_laps, live_laps, lse_laps, d_context_laps)
    )
    d_query = dquery_laps.reshape(tok_rows, model_width)
    grad_parts = grad_window.reshape(span_devs, tok_rows, 2 * model_width)
    kv_total = grad_parts[reach_devs]
    for offset in range(-reach_devs, reach_devs + 1):
        if offset != 0:
            kv_total = kv_total + shifted(
                grad_parts[reach_devs + offset].astype(jnp.bfloat16), "seq", offset
            ).astype(jnp.float32)
    d_projected = jnp.concatenate([d_query, kv_total.astype(jnp.bfloat16)], 1)
    qkv_part = jnp.einsum("td,te->de", input_one, d_projected, preferred_element_type=jnp.float32)
    d_norm1 = jnp.dot(d_projected, w_qkv.T, preferred_element_type=jnp.float32)
    d_first, gain_one_part, bias_one_part = norm_back(d_norm1, normed_one, inv_one, ln1_gain)
    tokens_grad = (d_hidden + d_first).astype(jnp.bfloat16)
    (
        qkv_grad,
        out_proj_grad,
        in_grad,
        back_grad,
        ln1_gain_grad,
        ln1_bias_grad,
        ln2_gain_grad,
        ln2_bias_grad,
    ) = (
        lax.psum_scatter(qkv_part, "seq", scatter_dimension=0, tiled=True),
        lax.psum_scatter(out_part, "seq", scatter_dimension=0, tiled=True),
        lax.psum_scatter(in_part, "seq", scatter_dimension=0, tiled=True),
        lax.psum_scatter(back_part, "seq", scatter_dimension=0, tiled=True),
        lax.psum_scatter(gain_one_part, "seq", scatter_dimension=0, tiled=True),
        lax.psum_scatter(bias_one_part, "seq", scatter_dimension=0, tiled=True),
        lax.psum_scatter(gain_two_part, "seq", scatter_dimension=0, tiled=True),
        lax.psum_scatter(bias_two_part, "seq", scatter_dimension=0, tiled=True),
    )
    (
        qkv_grad,
        out_proj_grad,
        in_grad,
        back_grad,
        ln1_gain_grad,
        ln1_bias_grad,
        ln2_gain_grad,
        ln2_bias_grad,
    ) = (
        lax.psum(qkv_grad.astype(jnp.bfloat16), "grp").astype(jnp.float32),
        lax.psum(out_proj_grad.astype(jnp.bfloat16), "grp").astype(jnp.float32),
        lax.psum(in_grad.astype(jnp.bfloat16), "grp").astype(jnp.float32),
        lax.psum(back_grad.astype(jnp.bfloat16), "grp").astype(jnp.float32),
        lax.psum(ln1_gain_grad.astype(jnp.bfloat16), "grp").astype(jnp.float32),
        lax.psum(ln1_bias_grad.astype(jnp.bfloat16), "grp").astype(jnp.float32),
        lax.psum(ln2_gain_grad.astype(jnp.bfloat16), "grp").astype(jnp.float32),
        lax.psum(ln2_bias_grad.astype(jnp.bfloat16), "grp").astype(jnp.float32),
    )
    return (
        output[None],
        tokens_grad[None],
        qkv_grad,
        out_proj_grad,
        in_grad,
        back_grad,
        ln1_gain_grad,
        ln1_bias_grad,
        ln2_gain_grad,
        ln2_bias_grad,
    )


def solution(mesh):
    in_specs = (
        P("grp", "seq", None),
        P(),
        P(),
        P(),
        P(),
        P(),
        P(),
        P(),
        P(),
        P("grp", None),
        P("grp", None),
        P("grp", None, None),
        P("grp", "seq", None),
        P("grp", "seq", None),
    )
    out_specs = (
        P("grp", "seq", None),
        P("grp", "seq", None),
        P("seq", None),
        P("seq", None),
        P("seq", None),
        P("seq", None),
        P("seq"),
        P("seq"),
        P("seq"),
        P("seq"),
    )
    return jax.shard_map(body, mesh=mesh, in_specs=in_specs, out_specs=out_specs, check_vma=False)
```

profile of v0, /device:TPU:0, one launch (start us, length us, event | category | flops | bytes accessed | tf_op | source)
XLA Modules:
  0.0 2395.9 jit_solution(10746670965130082013)
XLA Ops:
  80.2 85.1 %collective-permute-done = bf16[512,1536]{1,0:T(8,128)(2,1)} collective-permute-done((bf16[512,1536]{1,0:T(8,128)(2,1)}, bf16[512,1536]{1,0:T(8,128)(2,1)}, u32[]{:S(2)}, u32[]{:S(2)}) %collective-permute-start) | collective-permute-done | bytes 1572896 | tf_op jit(solution)/shard_map/ppermute | solution.py:18
  190.5 70.3 %collective-permute-start.5 = (bf16[512,1536]{1,0:T(8,128)(2,1)}, bf16[512,1536]{1,0:T(8,128)(2,1)S(1)}, u32[]{:S(2)}, u32[]{:S(2)}) collective-permute-start(bf16[512,1536]{1,0:T(8,128)(2,1)} %slice.137), channel_id=1, source_target_pairs={{0,6},{2,8},{4,10},{6,12},{8,14},{10,16},{12,18},{14,20},{16,22},{... | collective-permute-start | bytes 4718600 | tf_op jit(solution)/shard_map/ppermute | solution.py:18
  263.5 21.2 collective-permute-start.6
  292.0 20.7 collective-permute-done.6
  330.1 108.0 %collective-permute-done.9 = bf16[512,1536]{1,0:T(8,128)(2,1)S(1)} collective-permute-done((bf16[512,1536]{1,0:T(8,128)(2,1)}, bf16[512,1536]{1,0:T(8,128)(2,1)S(1)}, u32[]{:S(2)}, u32[]{:S(2)}) %collective-permute-start.9) | collective-permute-done | bytes 1572896 | tf_op jit(solution)/shard_map/ppermute | solution.py:18
  443.2 51.5 %collective-permute-done.11 = bf16[512,1536]{1,0:T(8,128)(2,1)S(1)} collective-permute-done((bf16[512,1536]{1,0:T(8,128)(2,1)}, bf16[512,1536]{1,0:T(8,128)(2,1)S(1)}, u32[]{:S(2)}, u32[]{:S(2)}) %collective-permute-start.11) | collective-permute-done | bytes 1572896 | tf_op jit(solution)/shard_map/ppermute | solution.py:18
  511.9 81.9 %collective-permute-done.15 = bf16[512,1536]{1,0:T(8,128)(2,1)S(1)} collective-permute-done((bf16[512,1536]{1,0:T(8,128)(2,1)}, bf16[512,1536]{1,0:T(8,128)(2,1)S(1)}, u32[]{:S(2)}, u32[]{:S(2)}) %collective-permute-start.15) | collective-permute-done | bytes 1572896 | tf_op jit(solution)/shard_map/ppermute | solution.py:18
  595.1 84.8 %reshape.663 = bf16[136,64,2,12,64]{4,3,2,1,0:T(8,128)(2,1)} reshape(bf16[17,512,1536]{2,1,0:T(8,128)(2,1)} %bitcast_dynamic-update-slice_fusion) | data formatting | bytes 53477376 | tf_op jit(solution)/shard_map/reshape | solution.py:125
  679.9 41.9 %copy.209 = bf16[136,64,2,12,64]{4,1,3,2,0:T(8,128)(2,1)} copy(bf16[136,64,2,12,64]{4,3,2,1,0:T(8,128)(2,1)} %reshape.663) | data formatting | bytes 53477376 | tf_op jit(solution)/shard_map/reshape | solution.py:125
  721.8 18.4 gather_fusion
  740.2 21.7 fusion.115
  859.0 20.3 multiply_convert_fusion.1
  921.0 49.3 %fusion.45 = f32[8,512,12,64]{1,3,2,0:T(8,128)} fusion(bf16[8,64,12,64]{1,3,2,0:T(8,128)(2,1)} %copy.219, f32[8,12,64,512]{3,2,1,0:T(8,128)} %fusion.118, f32[8,12,64,512]{3,2,1,0:T(8,128)} %copy-done.1, f32[8,12,64]{2,1,0:T(8,128)} %log_add_fusion, pred[8,512]{1,0:T(8,128)(4,1)S(1)} %compare_and_fusion), kind=kOutput, calls=%fused_computation.50 | convolution fusion | flops 437262848 | bytes 38563840 | tf_op jit(solution)/shard_map/while/body/eval_jaxpr/bhqk,bqhd->bkhd/dot_general | solution.py:194
  970.3 18.1 copy.222
  988.4 18.4 copy.220
  1006.9 18.8 reshape.635
  1025.7 18.8 reshape.636
  1044.5 36.6 %pad_maximum_fusion = f32[64,64,2,12,64]{1,0,4,3,2:T(8,128)} fusion(f32[64,64,1,12,64]{1,0,4,3,2:T(8,128)} %reshape.636, f32[64,64,1,12,64]{1,0,4,3,2:T(8,128)} %reshape.635), kind=kLoop, calls=%fused_computation.4 | loop fusion | flops 6291456 | bytes 50331648 | tf_op jit(solution)/shard_map/while/body/eval_jaxpr/stack | solution.py:197
  1081.1 49.0 %copy.223 = f32[64,64,2,12,64]{4,1,3,2,0:T(8,128)} copy(f32[64,64,2,12,64]{1,0,4,3,2:T(8,128)} %pad_maximum_fusion) | data formatting | bytes 50331648 | tf_op jit(solution)/shard_map/while/body/eval_jaxpr/stack | solution.py:197
  1130.1 33.2 %broadcast_in_dim.109 = f32[136,64,2,12,64]{4,1,3,2,0:T(8,128)} broadcast(f32[]{:T(128)} %constant.46.clone.1), dimensions={} | broadcast | bytes 53477380 | tf_op jit(solution)/shard_map/broadcast_in_dim | solution.py:207
  1163.3 113.5 %scatter_fusion = f32[136,64,2,12,64]{4,1,3,2,0:T(8,128)} fusion(f32[136,64,2,12,64]{4,1,3,2,0:T(8,128)} %broadcast_in_dim.109, s32[64]{0:T(128)S(1)} %copy-done.33, f32[64,64,2,12,64]{4,1,3,2,0:T(8,128)} %copy.223), kind=kCustom, calls=%fused_computation.2 | custom fusion | flops 6291456 | bytes 75497728 | tf_op jit(solution)/shard_map/while/body/eval_jaxpr/scatter-add | solution.py:204
  1276.8 51.5 %convert.23 = bf16[136,64,2,12,64]{4,1,3,2,0:T(8,128)(2,1)} convert(f32[136,64,2,12,64]{4,1,3,2,0:T(8,128)} %scatter_fusion) | non-fusion elementwise | flops 13369344 | bytes 80216064 | tf_op jit(solution)/shard_map/convert.15
  1328.3 35.1 %fusion.114 = (bf16[8,64,2,12,64]{4,1,3,2,0:T(8,128)(2,1)}, bf16[8,64,2,12,64]{4,1,3,2,0:T(8,128)(2,1)}, bf16[8,64,2,12,64]{4,1,3,2,0:T(8,128)(2,1)}, bf16[8,64,...) fusion(bf16[136,64,2,12,64]{4,1,3,2,0:T(8,128)(2,1)} %convert.23), kind=kLoop, calls=%fused_computation.184 | loop fusion | bytes 50331648 | tf_op jit(solution)/shard_map/slice | solution.py:217
  1505.3 22.8 collective-permute-done.28
  1529.4 32.4 %collective-permute-done.27 = bf16[512,1536]{0,1:T(8,128)(2,1)} collective-permute-done((bf16[512,1536]{0,1:T(8,128)(2,1)}, bf16[512,1536]{0,1:T(8,128)(2,1)}, u32[]{:S(2)}, u32[]{:S(2)}) %collective-permute-start.27) | collective-permute-done | bytes 1572896 | tf_op jit(solution)/shard_map/ppermute | solution.py:18
  1631.7 48.6 %fusion.71 = bf16[8,64,12,64]{1,3,2,0:T(8,128)(2,1)} fusion(bf16[8,512,12,64]{1,3,2,0:T(8,128)(2,1)} %squeeze.70, f32[8,12,64,512]{3,2,1,0:T(8,128)} %fusion.118, f32[8,12,64,512]{3,2,1,0:T(8,128)} %copy-done.1, f32[8,12,64]{2,1,0:T(8,128)} %log_add_fusion, pred[8,512]{1,0:T(8,128)(4,1)S(1)} %copy-done.14), kind=kOutput, calls=%fused_computation.99 | convolution fusion | flops 437656064 | bytes 32272384 | tf_op jit(solution)/shard_map/while/body/eval_jaxpr/bhqk,bkhd->bqhd/dot_general | solution.py:191
  1710.8 113.4 %collective-permute-done.18 = bf16[512,1536]{0,1:T(8,128)(2,1)} collective-permute-done((bf16[512,1536]{0,1:T(8,128)(2,1)}, bf16[512,1536]{0,1:T(8,128)(2,1)}, u32[]{:S(2)}, u32[]{:S(2)}) %collective-permute-start.18) | collective-permute-done | bytes 1572896 | tf_op jit(solution)/shard_map/ppermute | solution.py:18
  1824.2 21.5 collective-permute-done.17
  1891.9 172.6 %reduce-scatter.5.cloned.1.call-done = f32[48,2304]{1,0:T(8,128)} async-done(((f32[768,2304]{1,0:T(8,128)}), f32[48,2304]{1,0:T(8,128)}) %reduce-scatter.5.cloned.1.call-update) | async-done | bytes 442384 | tf_op jit(solution)/shard_map/reduce_scatter | solution.py:234
  2066.2 113.3 %reduce-scatter.9.cloned.1.call-done = f32[48,3072]{1,0:T(8,128)} async-done(((f32[768,3072]{1,0:T(8,128)}), f32[48,3072]{1,0:T(8,128)}) %reduce-scatter.9.cloned.1.call-update) | async-done | bytes 589840 | tf_op jit(solution)/shard_map/reduce_scatter | solution.py:236
  2181.3 113.9 %reduce-scatter.11.cloned.1.call-done = f32[192,768]{1,0:T(8,128)} async-done(((f32[3072,768]{1,0:T(8,128)}), f32[192,768]{1,0:T(8,128)}) %reduce-scatter.11.cloned.1.call-update) | async-done | bytes 589840 | tf_op jit(solution)/shard_map/reduce_scatter | solution.py:237
  2302.9 60.2 %all-reduce.4 = (bf16[768]{0:T(1024)(128)(2,1)}, bf16[768]{0:T(1024)(128)(2,1)}, bf16[768]{0:T(1024)(128)(2,1)}, bf16[768]{0:T(1024)(128)(2,1)}) all-reduce(f32[768]{0:T(1024)} %get-tuple-element.51, f32[768]{0:T(1024)} %get-tuple-element.65, f32[768]{0:T(1024)S(1)} %copy-done.29, ...), channel_id=6, replica_groups=mesh['seq'=16,'grp'=2] {'seq'}, use_global_device_ids=true, to_apply=%region_28.29.clone | all-reduce | flops 3072 | bytes 18432
  (320 shorter events, 613.6 us)
Async XLA Ops:
  7.2 1883.2 %reduce-scatter.7.cloned.1.call-start = ((), (), s32[]{:S(2)}) async-start(), calls=%async_computation.5 | async-start | bytes 2506752 | tf_op jit(solution)/shard_map/reduce_scatter | solution.py:235
  16.3 492.9 %collective-permute-start.14 = (bf16[512,1536]{1,0:T(8,128)(2,1)}, bf16[512,1536]{1,0:T(8,128)(2,1)}, u32[]{:S(2)}, u32[]{:S(2)}) collective-permute-start(bf16[512,1536]{1,0:T(8,128)(2,1)} %slice.137), channel_id=1, source_target_pairs={{14,0},{16,2},{18,4},{20,6},{22,8},{24,10},{26,12},{28,14},{30,16}... | collective-permute-start | bytes 4718600 | tf_op jit(solution)/shard_map/ppermute | solution.py:18
  17.6 489.0 %collective-permute-start.13 = (bf16[512,1536]{1,0:T(8,128)(2,1)}, bf16[512,1536]{1,0:T(8,128)(2,1)}, u32[]{:S(2)}, u32[]{:S(2)}) collective-permute-start(bf16[512,1536]{1,0:T(8,128)(2,1)} %slice.137), channel_id=1, source_target_pairs={{12,0},{14,2},{16,4},{18,6},{20,8},{22,10},{24,12},{26,14},{28,16}... | collective-permute-start | bytes 4718600 | tf_op jit(solution)/shard_map/ppermute | solution.py:18
  18.9 171.7 %collective-permute-start.2 = (bf16[512,1536]{1,0:T(8,128)(2,1)}, bf16[512,1536]{1,0:T(8,128)(2,1)}, u32[]{:S(2)}, u32[]{:S(2)}) collective-permute-start(bf16[512,1536]{1,0:T(8,128)(2,1)} %slice.137), channel_id=1, source_target_pairs={{0,12},{2,14},{4,16},{6,18},{8,20},{10,22},{12,24},{14,26},{16,28}... | collective-permute-start | bytes 4718600 | tf_op jit(solution)/shard_map/ppermute | solution.py:18
  26.5 159.5 %collective-permute-start.1 = (bf16[512,1536]{1,0:T(8,128)(2,1)}, bf16[512,1536]{1,0:T(8,128)(2,1)}, u32[]{:S(2)}, u32[]{:S(2)}) collective-permute-start(bf16[512,1536]{1,0:T(8,128)(2,1)} %slice.137), channel_id=1, source_target_pairs={{0,14},{2,16},{4,18},{6,20},{8,22},{10,24},{12,26},{14,28},{16,30}... | collective-permute-start | bytes 4718600 | tf_op jit(solution)/shard_map/ppermute | solution.py:18
  34.0 131.4 %collective-permute-start = (bf16[512,1536]{1,0:T(8,128)(2,1)}, bf16[512,1536]{1,0:T(8,128)(2,1)}, u32[]{:S(2)}, u32[]{:S(2)}) collective-permute-start(bf16[512,1536]{1,0:T(8,128)(2,1)} %slice.137), channel_id=1, source_target_pairs={{0,16},{2,18},{4,20},{6,22},{8,24},{10,26},{12,28},{14,30},{1,17},... | collective-permute-start | bytes 4718600 | tf_op jit(solution)/shard_map/ppermute | solution.py:18
  165.3 98.2 %collective-permute-start.3 = (bf16[512,1536]{1,0:T(8,128)(2,1)}, bf16[512,1536]{1,0:T(8,128)(2,1)S(1)}, u32[]{:S(2)}, u32[]{:S(2)}) collective-permute-start(bf16[512,1536]{1,0:T(8,128)(2,1)} %slice.137), channel_id=1, source_target_pairs={{0,10},{2,12},{4,14},{6,16},{8,18},{10,20},{12,22},{14,24},{16,26}... | collective-permute-start | bytes 4718600 | tf_op jit(solution)/shard_map/ppermute | solution.py:18
  186.0 99.9 %collective-permute-start.4 = (bf16[512,1536]{1,0:T(8,128)(2,1)}, bf16[512,1536]{1,0:T(8,128)(2,1)S(1)}, u32[]{:S(2)}, u32[]{:S(2)}) collective-permute-start(bf16[512,1536]{1,0:T(8,128)(2,1)} %slice.137), channel_id=1, source_target_pairs={{0,8},{2,10},{4,12},{6,14},{8,16},{10,18},{12,20},{14,22},{16,24},... | collective-permute-start | bytes 4718600 | tf_op jit(solution)/shard_map/ppermute | solution.py:18
  190.5 98.8 %collective-permute-start.5 = (bf16[512,1536]{1,0:T(8,128)(2,1)}, bf16[512,1536]{1,0:T(8,128)(2,1)S(1)}, u32[]{:S(2)}, u32[]{:S(2)}) collective-permute-start(bf16[512,1536]{1,0:T(8,128)(2,1)} %slice.137), channel_id=1, source_target_pairs={{0,6},{2,8},{4,10},{6,12},{8,14},{10,16},{12,18},{14,20},{16,22},{... | collective-permute-start | bytes 4718600 | tf_op jit(solution)/shard_map/ppermute | solution.py:18
  289.3 151.4 %collective-permute-start.10 = (bf16[512,1536]{1,0:T(8,128)(2,1)}, bf16[512,1536]{1,0:T(8,128)(2,1)S(1)}, u32[]{:S(2)}, u32[]{:S(2)}) collective-permute-start(bf16[512,1536]{1,0:T(8,128)(2,1)} %slice.137), channel_id=1, source_target_pairs={{6,0},{8,2},{10,4},{12,6},{14,8},{16,10},{18,12},{20,14},{22,16},{... | collective-permute-start | bytes 4718600 | tf_op jit(solution)/shard_map/ppermute | solution.py:18
  315.2 122.9 %collective-permute-start.9 = (bf16[512,1536]{1,0:T(8,128)(2,1)}, bf16[512,1536]{1,0:T(8,128)(2,1)S(1)}, u32[]{:S(2)}, u32[]{:S(2)}) collective-permute-start(bf16[512,1536]{1,0:T(8,128)(2,1)} %slice.137), channel_id=1, source_target_pairs={{4,0},{6,2},{8,4},{10,6},{12,8},{14,10},{16,12},{18,14},{20,16},{2... | collective-permute-start | bytes 4718600 | tf_op jit(solution)/shard_map/ppermute | solution.py:18
  327.5 167.2 %collective-permute-start.11 = (bf16[512,1536]{1,0:T(8,128)(2,1)}, bf16[512,1536]{1,0:T(8,128)(2,1)S(1)}, u32[]{:S(2)}, u32[]{:S(2)}) collective-permute-start(bf16[512,1536]{1,0:T(8,128)(2,1)} %slice.137), channel_id=1, source_target_pairs={{8,0},{10,2},{12,4},{14,6},{16,8},{18,10},{20,12},{22,14},{24,16},... | collective-permute-start | bytes 4718600 | tf_op jit(solution)/shard_map/ppermute | solution.py:18
  440.7 153.2 %collective-permute-start.15 = (bf16[512,1536]{1,0:T(8,128)(2,1)}, bf16[512,1536]{1,0:T(8,128)(2,1)S(1)}, u32[]{:S(2)}, u32[]{:S(2)}) collective-permute-start(bf16[512,1536]{1,0:T(8,128)(2,1)} %slice.137), channel_id=1, source_target_pairs={{16,0},{18,2},{20,4},{22,6},{24,8},{26,10},{28,12},{30,14},{17,1},... | collective-permute-start | bytes 4718600 | tf_op jit(solution)/shard_map/ppermute | solution.py:18
  1374.1 67.8 %collective-permute-start.16 = (bf16[512,1536]{0,1:T(8,128)(2,1)}, bf16[512,1536]{0,1:T(8,128)(2,1)}, u32[]{:S(2)}, u32[]{:S(2)}) collective-permute-start(bf16[512,1536]{0,1:T(8,128)(2,1)} %convert_element_type.242), channel_id=1, source_target_pairs={{16,0},{18,2},{20,4},{22,6},{24,8},{26,10},{28,12},{30,14},{17,1},... | collective-permute-start | bytes 4718600 | tf_op jit(solution)/shard_map/ppermute | solution.py:18
  1385.7 110.3 %collective-permute-start.31 = (bf16[512,1536]{0,1:T(8,128)(2,1)}, bf16[512,1536]{0,1:T(8,128)(2,1)}, u32[]{:S(2)}, u32[]{:S(2)}) collective-permute-start(bf16[512,1536]{0,1:T(8,128)(2,1)} %convert_element_type.272), channel_id=1, source_target_pairs={{0,16},{2,18},{4,20},{6,22},{8,24},{10,26},{12,28},{14,30},{1,17},... | collective-permute-start | bytes 4718600 | tf_op jit(solution)/shard_map/ppermute | solution.py:18
  1403.7 95.2 %collective-permute-start.30 = (bf16[512,1536]{0,1:T(8,128)(2,1)}, bf16[512,1536]{0,1:T(8,128)(2,1)}, u32[]{:S(2)}, u32[]{:S(2)}) collective-permute-start(bf16[512,1536]{0,1:T(8,128)(2,1)} %convert_element_type.270), channel_id=1, source_target_pairs={{0,14},{2,16},{4,18},{6,20},{8,22},{10,24},{12,26},{14,28},{16,30}... | collective-permute-start | bytes 4718600 | tf_op jit(solution)/shard_map/ppermute | solution.py:18
  1416.4 86.4 %collective-permute-start.29 = (bf16[512,1536]{0,1:T(8,128)(2,1)}, bf16[512,1536]{0,1:T(8,128)(2,1)}, u32[]{:S(2)}, u32[]{:S(2)}) collective-permute-start(bf16[512,1536]{0,1:T(8,128)(2,1)} %convert_element_type.268), channel_id=1, source_target_pairs={{0,12},{2,14},{4,16},{6,18},{8,20},{10,22},{12,24},{14,26},{16,28}... | collective-permute-start | bytes 4718600 | tf_op jit(solution)/shard_map/ppermute | solution.py:18
  1429.2 98.9 %collective-permute-start.28 = (bf16[512,1536]{0,1:T(8,128)(2,1)}, bf16[512,1536]{0,1:T(8,128)(2,1)}, u32[]{:S(2)}, u32[]{:S(2)}) collective-permute-start(bf16[512,1536]{0,1:T(8,128)(2,1)} %convert_element_type.266), channel_id=1, source_target_pairs={{0,10},{2,12},{4,14},{6,16},{8,18},{10,20},{12,22},{14,24},{16,26}... | collective-permute-start | bytes 4718600 | tf_op jit(solution)/shard_map/ppermute | solution.py:18
  1441.9 119.9 %collective-permute-start.27 = (bf16[512,1536]{0,1:T(8,128)(2,1)}, bf16[512,1536]{0,1:T(8,128)(2,1)}, u32[]{:S(2)}, u32[]{:S(2)}) collective-permute-start(bf16[512,1536]{0,1:T(8,128)(2,1)} %convert_element_type.264), channel_id=1, source_target_pairs={{0,8},{2,10},{4,12},{6,14},{8,16},{10,18},{12,20},{14,22},{16,24},... | collective-permute-start | bytes 4718600 | tf_op jit(solution)/shard_map/ppermute | solution.py:18
  1495.9 118.8 %collective-permute-start.26 = (bf16[512,1536]{0,1:T(8,128)(2,1)}, bf16[512,1536]{0,1:T(8,128)(2,1)}, u32[]{:S(2)}, u32[]{:S(2)}) collective-permute-start(bf16[512,1536]{0,1:T(8,128)(2,1)} %convert_element_type.262), channel_id=1, source_target_pairs={{0,6},{2,8},{4,10},{6,12},{8,14},{10,16},{12,18},{14,20},{16,22},{... | collective-permute-start | bytes 4718600 | tf_op jit(solution)/shard_map/ppermute | solution.py:18
  1499.0 117.1 %collective-permute-start.25 = (bf16[512,1536]{0,1:T(8,128)(2,1)}, bf16[512,1536]{0,1:T(8,128)(2,1)}, u32[]{:S(2)}, u32[]{:S(2)}) collective-permute-start(bf16[512,1536]{0,1:T(8,128)(2,1)} %convert_element_type.260), channel_id=1, source_target_pairs={{0,4},{2,6},{4,8},{6,10},{8,12},{10,14},{12,16},{14,18},{16,20},{1... | collective-permute-start | bytes 4718600 | tf_op jit(solution)/shard_map/ppermute | solution.py:18
  1502.8 114.5 %collective-permute-start.24 = (bf16[512,1536]{0,1:T(8,128)(2,1)}, bf16[512,1536]{0,1:T(8,128)(2,1)}, u32[]{:S(2)}, u32[]{:S(2)}) collective-permute-start(bf16[512,1536]{0,1:T(8,128)(2,1)} %convert_element_type.258), channel_id=1, source_target_pairs={{0,2},{2,4},{4,6},{6,8},{8,10},{10,12},{12,14},{14,16},{16,18},{18... | collective-permute-start | bytes 4718600 | tf_op jit(solution)/shard_map/ppermute | solution.py:18
  1528.1 90.5 %collective-permute-start.23 = (bf16[512,1536]{0,1:T(8,128)(2,1)}, bf16[512,1536]{0,1:T(8,128)(2,1)}, u32[]{:S(2)}, u32[]{:S(2)}) collective-permute-start(bf16[512,1536]{0,1:T(8,128)(2,1)} %convert_element_type.256), channel_id=1, source_target_pairs={{2,0},{4,2},{6,4},{8,6},{10,8},{12,10},{14,12},{16,14},{18,16},{20... | collective-permute-start | bytes 4718600 | tf_op jit(solution)/shard_map/ppermute | solution.py:18
  1614.8 85.7 %collective-permute-start.21 = (bf16[512,1536]{0,1:T(8,128)(2,1)}, bf16[512,1536]{0,1:T(8,128)(2,1)}, u32[]{:S(2)}, u32[]{:S(2)}) collective-permute-start(bf16[512,1536]{0,1:T(8,128)(2,1)} %convert_element_type.252), channel_id=1, source_target_pairs={{6,0},{8,2},{10,4},{12,6},{14,8},{16,10},{18,12},{20,14},{22,16},{... | collective-permute-start | bytes 4718600 | tf_op jit(solution)/shard_map/ppermute | solution.py:18
  1616.1 87.8 %collective-permute-start.20 = (bf16[512,1536]{0,1:T(8,128)(2,1)}, bf16[512,1536]{0,1:T(8,128)(2,1)}, u32[]{:S(2)}, u32[]{:S(2)}) collective-permute-start(bf16[512,1536]{0,1:T(8,128)(2,1)} %convert_element_type.250), channel_id=1, source_target_pairs={{8,0},{10,2},{12,4},{14,6},{16,8},{18,10},{20,12},{22,14},{24,16},... | collective-permute-start | bytes 4718600 | tf_op jit(solution)/shard_map/ppermute | solution.py:18
  1617.4 93.4 %collective-permute-start.19 = (bf16[512,1536]{0,1:T(8,128)(2,1)}, bf16[512,1536]{0,1:T(8,128)(2,1)}, u32[]{:S(2)}, u32[]{:S(2)}) collective-permute-start(bf16[512,1536]{0,1:T(8,128)(2,1)} %convert_element_type.248), channel_id=1, source_target_pairs={{10,0},{12,2},{14,4},{16,6},{18,8},{20,10},{22,12},{24,14},{26,16}... | collective-permute-start | bytes 4718600 | tf_op jit(solution)/shard_map/ppermute | solution.py:18
  1618.7 205.5 %collective-permute-start.18 = (bf16[512,1536]{0,1:T(8,128)(2,1)}, bf16[512,1536]{0,1:T(8,128)(2,1)}, u32[]{:S(2)}, u32[]{:S(2)}) collective-permute-start(bf16[512,1536]{0,1:T(8,128)(2,1)} %convert_element_type.246), channel_id=1, source_target_pairs={{12,0},{14,2},{16,4},{18,6},{20,8},{22,10},{24,12},{26,14},{28,16}... | collective-permute-start | bytes 4718600 | tf_op jit(solution)/shard_map/ppermute | solution.py:18
  1620.0 225.7 %collective-permute-start.17 = (bf16[512,1536]{0,1:T(8,128)(2,1)}, bf16[512,1536]{0,1:T(8,128)(2,1)}, u32[]{:S(2)}, u32[]{:S(2)}) collective-permute-start(bf16[512,1536]{0,1:T(8,128)(2,1)} %convert_element_type.244), channel_id=1, source_target_pairs={{14,0},{16,2},{18,4},{20,6},{22,8},{24,10},{26,12},{28,14},{30,16}... | collective-permute-start | bytes 4718600 | tf_op jit(solution)/shard_map/ppermute | solution.py:18
  1625.2 439.3 %reduce-scatter.5.cloned.1.call-start = ((), (), s32[]{:S(2)}) async-start(), calls=%async_computation.4 | async-start | bytes 7520256 | tf_op jit(solution)/shard_map/reduce_scatter | solution.py:234
  1863.2 316.3 %reduce-scatter.9.cloned.1.call-start = ((), (), s32[]{:S(2)}) async-start(), calls=%async_computation.6 | async-start | bytes 10027008 | tf_op jit(solution)/shard_map/reduce_scatter | solution.py:236
  1872.8 422.4 %reduce-scatter.11.cloned.1.call-start = ((), (), s32[]{:S(2)}) async-start(), calls=%async_computation.7 | async-start | bytes 10027008 | tf_op jit(solution)/shard_map/reduce_scatter | solution.py:237
  1881.3 501.0 %all-reduce.9.cloned.1.call-start = ((), (), s32[]{:S(2)}) async-start(), calls=%async_computation.8 | async-start | bytes 1769472 | tf_op jit(solution)/shard_map/psum | solution.py:253
  (51 other events, 2451.9 us)
Sparse Core Ops, SparseCore 0:
  1625.3 255.7 reduce-scatter.6
  1885.6 178.7 reduce-scatter.4
  2068.6 110.8 reduce-scatter.8
  2184.0 111.1 reduce-scatter.10
  2298.1 36.7 all-reduce.8
where the time goes:
time: 2410 us; the launch traced here: 2400 us
  waiting for transfers between devices  965 us (40%)
  local copies, waits for them, and re-layouts  704 us (29%)
  other arithmetic  260 us (11%)
  matrix products  207 us (9%)
  starting transfers between devices  179 us (7%)
  blocking collectives  65.8 us (3%)
    ppermute x32, waiting for transfers between devices, shifted(): return lax.ppermute(block, axis, route)  565 us
    ppermute x32, starting transfers between devices, shifted(): return lax.ppermute(block, axis, route)  178 us
    reduce_scatter x1, waiting for transfers between devices, body(): lax.psum_scatter(qkv_part, 'seq', scatter_dimension=0, tiled=True)  173 us
    reshape x2, local copies, waits for them, and re-layouts, body(): jnp.stack(pieces).reshape(span_devs * per_dev, BLK, 2, head_count, HD)  127 us
    slice x17, local copies, waits for them, and re-layouts, body(): grad_parts[reach_devs + offset].astype(jnp.bfloat16)  114 us
    reduce_scatter x1, waiting for transfers between devices, body(): lax.psum_scatter(back_part, 'seq', scatter_dimension=0, tiled=True)  114 us
    scatter-add x1, other arithmetic, backward_lap(): grad_window.at[ids.reshape(lap_blocks * cand_count)].add(d_gathered)  114 us
    reduce_scatter x1, waiting for transfers between devices, body(): lax.psum_scatter(in_part, 'seq', scatter_dimension=0, tiled=True)  113 us
  transfers between devices with their start and end apart: 37, of which 16 were waited for; matrix products, arithmetic and copies ran while one was open for 15% of the time, Pallas kernels for 0%

commit v1 on v0

v1 whole, which is shorter than its diff:
```python
import functools

import jax
import jax.numpy as jnp
from jax import lax
from jax.experimental import pallas as pl
from jax.experimental.pallas import tpu as pltpu
from jax.sharding import PartitionSpec as P

HD = 64
BLK = 64
UNITB = 8
QUAD = 4
QW = QUAD * HD
ln_eps = 1e-12
bf16 = jnp.bfloat16
f32 = jnp.float32
VMEM_LIMIT = 60 * 1024 * 1024
vmem = functools.partial(pl.BlockSpec, memory_space=pltpu.VMEM)
smem = functools.partial(pl.BlockSpec, memory_space=pltpu.SMEM)
anym = functools.partial(pl.BlockSpec, memory_space=pl.ANY)


def shape(dims, dtype):
    return jax.ShapeDtypeStruct(dims, dtype)


def dot(a, b):
    return lax.dot_general(a, b, (((1,), (0,)), ((), ())), preferred_element_type=f32)


def dot_nt(a, b):
    return lax.dot_general(a, b, (((1,), (1,)), ((), ())), preferred_element_type=f32)


def dot_tn(a, b):
    return lax.dot_general(a, b, (((0,), (0,)), ((), ())), preferred_element_type=f32)


def norm_stats(values):
    center = values - jnp.mean(values, -1, keepdims=True)
    inv_std = lax.rsqrt(jnp.mean(center * center, -1, keepdims=True) + ln_eps)
    return center * inv_std, inv_std


def block_plan(doc_len, tail_len, global_rel, rand_rows, first_row):
    per_dev = rand_rows.shape[0]
    doc_end = jnp.cumsum(doc_len) * UNITB
    starts = doc_end - doc_len * UNITB
    mine = ((first_row >= starts) & (first_row < doc_end)).astype(jnp.int32)
    begin = jnp.sum(mine * starts)
    finish = jnp.sum(mine * doc_end)
    padding = jnp.sum(mine * tail_len)
    glob_one = begin + jnp.sum(mine * global_rel[:, 0])
    glob_two = begin + jnp.sum(mine * global_rel[:, 1])
    rows = first_row + jnp.arange(per_dev, dtype=jnp.int32)
    before = jnp.where(rows - 1 >= begin, rows - 1, -1)
    follow = jnp.where(rows + 1 < finish, rows + 1, -1)
    whole = jnp.zeros_like(rows)
    candidates = jnp.concatenate(
        [jnp.stack([before, rows, follow, whole + glob_one, whole + glob_two], 1), rand_rows], 1
    )
    count = candidates.shape[1]
    equal = candidates[:, :, None] == candidates[:, None, :]
    earlier = jnp.arange(count)[:, None] > jnp.arange(count)[None, :]
    usable = (candidates >= 0) & jnp.logical_not(jnp.any(equal & earlier[None], 2))
    filled = jnp.where(candidates == finish - 1, BLK - padding, BLK)
    live = jnp.where(usable, filled, 0).astype(jnp.int32)
    halo = jnp.stack(
        [
            jnp.where(first_row - 1 >= begin, first_row - 1, first_row),
            jnp.where(first_row + per_dev < finish, first_row + per_dev, first_row),
            glob_one,
            glob_two,
        ]
    )
    slots = jnp.concatenate([halo, rand_rows.reshape(-1)]).astype(jnp.int32)
    return live.reshape(-1), slots


def head_masks(rows):
    lane = lax.broadcasted_iota(jnp.int32, (rows, QW), 1) // HD
    return [lane == h for h in range(QUAD)]


def spread(values, masks):
    zero = jnp.zeros_like(values)
    return jnp.concatenate([jnp.where(m, values, zero) for m in masks], 0)


def collect(values, masks):
    out = values[:BLK]
    for h in range(1, QUAD):
        out = jnp.where(masks[h], values[h * BLK : (h + 1) * BLK], out)
    return out


def key_rows(ext, slots, i, cols):
    return jnp.concatenate(
        [
            ext[pl.ds(pl.multiple_of(i * BLK, BLK), 3 * BLK), cols],
            slots[2 * BLK : 4 * BLK, cols],
            slots[pl.ds(pl.multiple_of((4 + 3 * i) * BLK, BLK), 3 * BLK), cols],
        ],
        0,
    )


def masked(scores, live, i, cand):
    row = lax.broadcasted_iota(jnp.int32, (BLK, QW), 0)
    return jnp.concatenate(
        [
            jnp.where(row < live[i * cand + c], scores[c * BLK : (c + 1) * BLK], -1e30)
            for c in range(cand)
        ],
        0,
    )


def fill_ext(ext, own, slots):
    rows = own.shape[0]
    ext[0:BLK, :] = slots[0:BLK, :]
    ext[BLK : BLK + rows, :] = own[...]
    ext[BLK + rows : 2 * BLK + rows, :] = slots[BLK : 2 * BLK, :]


def forward_kernel(
    slot_ids, live, window, query, own_kv, w_qkv, gain, bias,
    context, lse, slot_norm, slot_kv,
    slot_tok, ext, sems,
):
    count = slot_tok.shape[0]
    width = query.shape[1]
    nblk = query.shape[0] // BLK
    cand = live.shape[0] // nblk

    def fetch(s):
        return pltpu.make_async_copy(window.at[slot_ids[s]], slot_tok.at[s], sems.at[s])

    for s in range(count):
        fetch(s).start()
    group = 4

    def project(step, _):
        for k in range(group):
            fetch(step * group + k).wait()
        rows = pl.ds(pl.multiple_of(step * group * BLK, group * BLK), group * BLK)
        tok = slot_tok[pl.ds(step * group, group)].reshape(group * BLK, width).astype(f32)
        normed, _ = norm_stats(tok)
        low = (normed * gain[...] + bias[...]).astype(bf16)
        slot_norm[rows, :] = low
        slot_kv[rows, :] = dot(low, w_qkv[:, width:]).astype(bf16)
        return 0

    lax.fori_loop(0, count // group, project, 0)
    fill_ext(ext, own_kv, slot_kv)
    masks = head_masks(BLK)

    def attend(i, _):
        qrows = pl.ds(pl.multiple_of(i * BLK, BLK), BLK)
        for quad in range(width // QW):
            cols = pl.ds(quad * QW, QW)
            vcols = pl.ds(width + quad * QW, QW)
            keys = key_rows(ext, slot_kv, i, cols)
            vals = key_rows(ext, slot_kv, i, vcols)
            scores = masked(dot_nt(keys, spread(query[qrows, cols], masks)), live, i, cand)
            top = jnp.max(scores, 0, keepdims=True)
            expo = jnp.exp(scores - top)
            total = jnp.sum(expo, 0, keepdims=True)
            probs = (expo * (1.0 / total)).astype(bf16)
            lse[i, pl.ds(quad, 1), :] = top + jnp.log(total)
            context[qrows, cols] = collect(dot_tn(probs, vals), masks).astype(bf16)
        return 0

    lax.fori_loop(0, nblk, attend, 0)


def backward_kernel(
    live, query, own_kv, slot_kv, lse, d_context, own_norm, slot_norm, w_qkv,
    d_own_norm, d_slot_norm, qkv_part,
    ext, d_ext, d_glob, d_slot, d_query,
):
    rows_own, width = query.shape
    nblk = rows_own // BLK
    cand = live.shape[0] // nblk
    fill_ext(ext, own_kv, slot_kv)
    d_ext[...] = jnp.zeros_like(d_ext)
    d_glob[...] = jnp.zeros_like(d_glob)
    masks = head_masks(BLK)

    def attend(i, _):
        qrows = pl.ds(pl.multiple_of(i * BLK, BLK), BLK)
        near = pl.ds(pl.multiple_of(i * BLK, BLK), 3 * BLK)
        far = pl.ds(pl.multiple_of((4 + 3 * i) * BLK, BLK), 3 * BLK)
        for quad in range(width // QW):
            cols = pl.ds(quad * QW, QW)
            vcols = pl.ds(width + quad * QW, QW)
            keys = key_rows(ext, slot_kv, i, cols)
            vals = key_rows(ext, slot_kv, i, vcols)
            spread_q = spread(query[qrows, cols], masks)
            spread_d = spread(d_context[qrows, cols], masks)
            scores = masked(dot_nt(keys, spread_q), live, i, cand)
            probs = jnp.exp(scores - lse[i, pl.ds(quad, 1), :])
            d_probs = dot_nt(vals, spread_d)
            delta = jnp.sum(d_probs * probs, 0, keepdims=True)
            d_scores = (probs * (d_probs - delta)).astype(bf16)
            d_keys = dot(d_scores, spread_q)
            d_vals = dot(probs.astype(bf16), spread_d)
            d_query[qrows, cols] = (collect(dot_tn(d_scores, keys), masks) * HD**-0.5).astype(bf16)
            for grads, where in ((d_keys, cols), (d_vals, vcols)):
                d_ext[near, where] += grads[: 3 * BLK]
                d_glob[:, where] += grads[3 * BLK : 5 * BLK]
                d_slot[far, where] = grads[5 * BLK :].astype(bf16)
        return 0

    lax.fori_loop(0, nblk, attend, 0)
    d_slot[0:BLK, :] = d_ext[0:BLK, :].astype(bf16)
    d_slot[BLK : 2 * BLK, :] = d_ext[BLK + rows_own :, :].astype(bf16)
    d_slot[2 * BLK : 4 * BLK, :] = d_glob[...].astype(bf16)
    ext[0:rows_own, :] = d_ext[BLK : BLK + rows_own, :].astype(bf16)
    d_own = ext[0:rows_own, :]
    d_own_norm[...] = dot_nt(d_query[...], w_qkv[:, :width]) + dot_nt(d_own, w_qkv[:, width:])
    step_rows = 4 * BLK

    def back(step, _):
        rows = pl.ds(pl.multiple_of(step * step_rows, step_rows), step_rows)
        d_slot_norm[rows, :] = dot_nt(d_slot[rows, :], w_qkv[:, width:])
        return 0

    lax.fori_loop(0, d_slot.shape[0] // step_rows, back, 0)
    dests, parts, share, _ = qkv_part.shape
    qkv_part[:, 0] = dot_tn(own_norm[...], d_query[...]).astype(bf16).reshape(dests, share, width)
    for part in range(1, parts):
        cols = pl.ds((part - 1) * width, width)
        grads = dot_tn(own_norm[...], d_own[:, (part - 1) * width : part * width])
        grads += dot_tn(slot_norm[...], d_slot[:, cols])
        qkv_part[:, part] = grads.astype(bf16).reshape(dests, share, width)


def gelu_both(x):
    half_erf = 0.5 * lax.erf(x * 0.7071067811865476)
    cdf = 0.5 + half_erf
    density = jnp.exp(-0.5 * x * x) * 0.3989422804014327
    return x * cdf, cdf + x * density


def middle_kernel(
    tokens, context, grad_out, w_out, gain, bias, w_in, w_back,
    output, d_hidden, d_context, in_part, back_part, out_part, gain_part, bias_part,
    hidden, norm_low, norm_t, out_sum, d_norm, act, slope,
):
    step, steps = pl.program_id(0), pl.num_programs(0)
    rows, width = hidden.shape
    tile = 128

    @pl.when(step == 0)
    def _():
        for r in range(0, rows, tile):
            t = slice(r, r + tile)
            value = tokens[t, :].astype(f32) + dot(context[t, :], w_out[...])
            hidden[t, :] = value
            normed, _ = norm_stats(value)
            norm_low[t, :] = (normed * gain[...] + bias[...]).astype(bf16)
        norm_t[...] = norm_low[...].T
        out_sum[...] = jnp.zeros_like(out_sum)
        d_norm[...] = jnp.zeros_like(d_norm)

    for r in range(0, rows, tile):
        t = slice(r, r + tile)
        value, grad = gelu_both(dot(norm_low[t, :], w_in[...]))
        low = value.astype(bf16)
        act[t, :] = low
        out_sum[t, :] += dot(low, w_back[...])
        d_low = (dot_nt(grad_out[t, :], w_back[...]) * grad).astype(bf16)
        slope[t, :] = d_low
        d_norm[t, :] += dot_nt(d_low, w_in[...])
    chunk = act.shape[1]
    back_part[...] = dot_tn(act[...], grad_out[...]).astype(bf16).reshape(back_part.shape)
    in_part[...] = dot(norm_t[...], slope[...]).astype(bf16).reshape(in_part.shape)

    @pl.when(step == steps - 1)
    def _():
        for r in range(0, rows, tile):
            t = slice(r, r + tile)
            value = hidden[t, :]
            output[t, :] = (value + out_sum[t, :]).astype(bf16)
            normed, inv = norm_stats(value)
            grad = d_norm[t, :]
            part_gain = jnp.sum(grad * normed, 0, keepdims=True)
            part_bias = jnp.sum(grad, 0, keepdims=True)
            if r == 0:
                gain_part[...] = part_gain
                bias_part[...] = part_bias
            else:
                gain_part[...] += part_gain
                bias_part[...] += part_bias
            hat = grad * gain[...]
            mean_hat = jnp.mean(hat, -1, keepdims=True)
            mean_dot = jnp.mean(hat * normed, -1, keepdims=True)
            total = grad_out[t, :].astype(f32) + inv * (hat - mean_hat - normed * mean_dot)
            d_hidden[t, :] = total
            low = total.astype(bf16)
            norm_low[t, :] = low
            d_context[t, :] = dot_nt(low, w_out[...]).astype(bf16)
        out_part[...] = dot_tn(context[...], norm_low[...]).astype(bf16)


def body(
    tokens, w_qkv, w_out, w_in, w_back, ln1_gain, ln1_bias, ln2_gain, ln2_bias,
    doc_units, tail_pad, global_ids, rand_blocks, out_grad,
):
    tok = tokens[0]
    grad_out = out_grad[0]
    rows, width = tok.shape
    ff = w_in.shape[1]
    per_dev = rows // BLK
    shards = lax.axis_size("seq")
    share = width // 16 if shards == 16 else width // shards
    first_row = lax.axis_index("seq") * per_dev
    live, slots = block_plan(doc_units[0], tail_pad[0], global_ids[0], rand_blocks[0], first_row)
    count = slots.shape[0]
    gain1, bias1 = ln1_gain[None], ln1_bias[None]
    gain2, bias2 = ln2_gain[None], ln2_bias[None]

    window = lax.all_gather(tok, "seq").reshape(shards * per_dev, BLK, width)

    normed_one, inv_one = norm_stats(tok.astype(f32))
    own_norm = (normed_one * ln1_gain + ln1_bias).astype(bf16)
    projected = jnp.dot(own_norm, w_qkv, preferred_element_type=f32)
    query = (projected[:, :width] * HD**-0.5).astype(bf16)
    own_kv = projected[:, width:].astype(bf16)

    params = pltpu.CompilerParams(vmem_limit_bytes=VMEM_LIMIT)
    quads = width // QW
    context, lse, slot_norm, slot_kv = pl.pallas_call(
        forward_kernel,
        out_shape=[
            shape((rows, width), bf16),
            shape((per_dev, quads, QW), f32),
            shape((count * BLK, width), bf16),
            shape((count * BLK, 2 * width), bf16),
        ],
        in_specs=[smem(), smem(), anym()] + [vmem()] * 5,
        out_specs=[vmem()] * 4,
        scratch_shapes=[
            pltpu.VMEM((count, BLK, width), bf16),
            pltpu.VMEM((rows + 2 * BLK, 2 * width), bf16),
            pltpu.SemaphoreType.DMA((count,)),
        ],
        compiler_params=params,
        name="attend_forward",
    )(slots, live, window, query, own_kv, w_qkv, gain1, bias1)

    chunk = width
    steps = ff // chunk
    per_share = ff // shards
    dests = chunk // per_share
    const = lambda *dims: pl.BlockSpec(dims, lambda s: (0,) * len(dims))
    output, d_hidden, d_context, in_part, back_part, out_part, gain_two, bias_two = pl.pallas_call(
        middle_kernel,
        grid=(steps,),
        in_specs=[
            const(rows, width), const(rows, width), const(rows, width), const(width, width),
            const(1, width), const(1, width),
            pl.BlockSpec((width, chunk), lambda s: (0, s)),
            pl.BlockSpec((chunk, width), lambda s: (s, 0)),
        ],
        out_specs=[
            const(rows, width), const(rows, width), const(rows, width),
            pl.BlockSpec((width, chunk), lambda s: (0, s)),
            pl.BlockSpec((chunk, width), lambda s: (s, 0)),
            const(width, width), const(1, width), const(1, width),
        ],
        out_shape=[
            shape((rows, width), bf16), shape((rows, width), f32), shape((rows, width), bf16),
            shape((width, ff), bf16), shape((ff, width), bf16), shape((width, width), bf16),
            shape((1, width), f32), shape((1, width), f32),
        ],
        scratch_shapes=[
            pltpu.VMEM((rows, width), f32), pltpu.VMEM((rows, width), bf16),
            pltpu.VMEM((width, rows), bf16), pltpu.VMEM((rows, width), f32),
            pltpu.VMEM((rows, width), f32), pltpu.VMEM((rows, chunk), bf16),
            pltpu.VMEM((rows, chunk), bf16),
        ],
        compiler_params=params,
        name="middle",
    )(tok, context, grad_out, w_out, gain2, bias2, w_in, w_back)

    parts = w_qkv.shape[1] // width
    d_own_norm, d_slot_norm, qkv_part = pl.pallas_call(
        backward_kernel,
        out_shape=[
            shape((rows, width), f32),
            shape((count * BLK, width), f32),
            shape((1, parts, width, width), bf16),
        ],
        in_specs=[smem()] + [vmem()] * 8,
        out_specs=[vmem()] * 3,
        scratch_shapes=[
            pltpu.VMEM((rows + 2 * BLK, 2 * width), bf16),
            pltpu.VMEM((rows + 2 * BLK, 2 * width), f32),
            pltpu.VMEM((2 * BLK, 2 * width), f32),
            pltpu.VMEM((count * BLK, 2 * width), bf16),
            pltpu.VMEM((rows, width), bf16),
        ],
        compiler_params=params,
        name="attend_backward",
    )(live, query, own_kv, slot_kv, lse, d_context, own_norm, slot_norm, w_qkv)

    spread_grads = jnp.zeros((shards * per_dev, BLK, width), f32)
    spread_grads = spread_grads.at[slots].add(d_slot_norm.reshape(count, BLK, width))
    others = lax.psum_scatter(
        spread_grads.astype(bf16).reshape(shards * rows, width), "seq", scatter_dimension=0, tiled=True
    )
    d_norm1 = d_own_norm + others.astype(f32)
    grad_hat = d_norm1 * ln1_gain
    d_first = inv_one * (
        grad_hat
        - jnp.mean(grad_hat, -1, keepdims=True)
        - normed_one * jnp.mean(grad_hat * normed_one, -1, keepdims=True)
    )
    tokens_grad = (d_hidden + d_first).astype(bf16)
    gain_one = jnp.sum(d_norm1 * normed_one, 0)
    bias_one = jnp.sum(d_norm1, 0)

    def reduce(part):
        mine = lax.psum_scatter(part, "seq", scatter_dimension=0, tiled=True)
        return lax.psum(mine, "grp").astype(f32)

    qkv_part = jnp.moveaxis(qkv_part[0], 0, 1).reshape(width, parts * width)
    vectors = jnp.stack([gain_one, bias_one, gain_two[0], bias_two[0]], 1)
    vectors = lax.psum(lax.psum_scatter(vectors, "seq", scatter_dimension=0, tiled=True), "grp")
    return (
        output[None],
        tokens_grad[None],
        reduce(qkv_part),
        reduce(out_part),
        reduce(in_part),
        reduce(back_part),
        vectors[:, 0],
        vectors[:, 1],
        vectors[:, 2],
        vectors[:, 3],
    )


def solution(mesh):
    in_specs = (
        P("grp", "seq", None),
        P(),
        P(),
        P(),
        P(),
        P(),
        P(),
        P(),
        P(),
        P("grp", None),
        P("grp", None),
        P("grp", None, None),
        P("grp", "seq", None),
        P("grp", "seq", None),
    )
    out_specs = (
        P("grp", "seq", None),
        P("grp", "seq", None),
        P("seq", None),
        P("seq", None),
        P("seq", None),
        P("seq", None),
        P("seq"),
        P("seq"),
        P("seq"),
        P("seq"),
    )
    return jax.shard_map(body, mesh=mesh, in_specs=in_specs, out_specs=out_specs, check_vma=False)
```

time: 2410 us -> 761 us (0.32)
  local copies, waits for them, and re-layouts: 704 us -> 36.5 us
  waiting for transfers between devices: 965 us -> 550 us
  other arithmetic: 260 us -> 48.2 us
  matrix products: 207 us -> 4.31 us
  starting transfers between devices: 179 us -> 0.31 us
  Pallas kernels: 0 us -> 96.5 us
  blocking collectives: 65.8 us -> 4.92 us
    ppermute x32 -> x0, waiting for transfers between devices: 565 us -> none  [shifted(): return lax.ppermute(block, axis, route)]
    dot_general x18 -> x1, matrix products: 207 us -> 4.31 us  [body(): projected = jnp.dot(own_norm, w_qkv, preferred_element_type=f32)]
    ppermute x32 -> x0, starting transfers between devices: 178 us -> none  [shifted(): return lax.ppermute(block, axis, route)]
    reshape x6 -> x0, local copies, waits for them, and re-layouts: 171 us -> none  [the longest x2 127 us: body(): jnp.stack(pieces).reshape(span_devs * per_dev, BLK, 2, head_count, HD)]
    slice x22 -> x1, local copies, waits for them, and re-layouts: 152 us -> 1.53 us  [body(): own_kv = projected[:, width:].astype(bf16)]
    unnamed x5 -> x10, waiting for transfers between devices: 0.08 us -> 119 us
    scatter-add x1, other arithmetic: 114 us -> 15.8 us  [body(): spread_grads.at[slots].add(d_slot_norm.reshape(count, BLK, width))]
    pallas_call x0 -> x3, Pallas kernels: none -> 96.5 us  [the longest x1 38 us: body(): pl.pallas_call(backward_kernel, out_shape=[shape((rows, width), f32), sha...]
  transfers between devices with their start and end apart: 37 -> 8, of which waited for: 16 -> 8; matrix products, arithmetic and copies ran while one was open for 15% -> 10% of each run, Pallas kernels for 0% -> 0%
where the time goes in v1:
time: 761 us; the launch traced here: 760 us
  waiting for transfers between devices  550 us (72%)
  Pallas kernels  96.5 us (13%)
  other arithmetic  48.2 us (6%)
  local copies, waits for them, and re-layouts  36.5 us (5%)
  between operations  19.6 us (3%)
    reduce_scatter x3, waiting for transfers between devices, reduce(): mine = lax.psum_scatter(part, 'seq', scatter_dimension=0, tiled=True)  216 us
    reduce_scatter x1, waiting for transfers between devices, body(): lax.psum_scatter(spread_grads.astype(bf16).reshape(shards * rows, width),...  132 us
    unnamed x10, waiting for transfers between devices  119 us
    all_gather x1, waiting for transfers between devices, body(): window = lax.all_gather(tok, 'seq').reshape(shards * per_dev, BLK, width)  78 us
    pallas_call x1, Pallas kernels, body(): pl.pallas_call(backward_kernel, out_shape=[shape((rows, width), f32), sha...  38 us
    pallas_call x1, Pallas kernels, body(): pl.pallas_call(middle_kernel, grid=(steps,), in_specs=[const(rows, width)...  32.3 us
    pallas_call x1, Pallas kernels, body(): pl.pallas_call(forward_kernel, out_shape=[shape((rows, width), bf16), sha...  26.3 us
    scatter-add x1, other arithmetic, body(): spread_grads.at[slots].add(d_slot_norm.reshape(count, BLK, width))  15.8 us
  transfers between devices with their start and end apart: 8, of which 8 were waited for; matrix products, arithmetic and copies ran while one was open for 10% of the time, Pallas kernels for 0%

profile of v1, /device:TPU:0, one launch (start us, length us, event | category | flops | bytes accessed | tf_op | source)
XLA Modules:
  0.0 760.4 jit_solution(2497902329000486072)
XLA Ops:
  8.8 1.5 fusion.19
  14.8 1.3 broadcast_in_dim.51.gain
  16.1 1.3 broadcast_in_dim.52.bias
  21.4 1.3 compare_select_fusion
  23.8 1.3 convert_reduce_fusion
  25.9 4.3 fusion.23
  30.2 1.5 slice.45.own_kv
  33.4 2.4 fusion.15.query
  35.8 78.0 %all-gather.2.cloned.1.call-done = bf16[16,512,768]{2,1,0:T(8,128)(2,1)} async-done(((bf16[1,512,768]{2,1,0:T(8,128)(2,1)}), bf16[16,512,768]{2,1,0:T(8,128)(2,1)}) %all-gather.2.cloned.1.call-update) | async-done | bytes 12582928 | tf_op jit(solution)/shard_map/all_gather | solution.py:325
  113.8 26.3 %attend_forward.1 = (bf16[512,768]{1,0:T(8,128)(2,1)}, f32[8,3,256]{2,1,0:T(4,128)}, bf16[1792,768]{1,0:T(8,128)(2,1)}, bf16[1792,1536]{1,0:T(8,128)(2,1)}) custom-call(s32[28]{0:T(128)} %concatenate.37.slot_ids, s32[64]{0:T(128)} %select_n.58.live, bf16[128,64,768]{2,1,0:T(8,128)(2,1)} %bitcast.76, bf16[512,768]{1,0:T(8,128)(2,1)} %fusion.15.query, ...), custom_call_target="tpu_custom_call" | custom-call | tf_op jit(solution)/shard_map/attend_forward/pallas_call | solution.py:335
  140.1 32.3 %middle.1 = (bf16[512,768]{1,0:T(8,128)(2,1)}, f32[512,768]{1,0:T(8,128)}, bf16[512,768]{1,0:T(8,128)(2,1)}, bf16[768,3072]{1,0:T(8,128)(2,1)}, bf16[3072,768]{1...) custom-call(bf16[512,768]{1,0:T(8,128)(2,1)} %bitcast.74, ...), custom_call_target="tpu_custom_call" | custom-call | tf_op jit(solution)/shard_map/middle/pallas_call | solution.py:359
  172.4 38.0 %attend_backward.1 = (f32[512,768]{1,0:T(8,128)}, f32[1792,768]{1,0:T(8,128)}, bf16[1,3,768,768]{3,2,1,0:T(8,128)(2,1)}) custom-call(s32[64]{0:T(128)} %select_n.58.live, bf16[512,768]{1,0:T(8,128)(2,1)} %fusion.15.query, bf16[512,1536]{1,0:T(8,128)(2,1)} %slice.45.own_kv, bf16[1792,1536]{1,0:T(8,128)(2,1)} %get-tuple-element.28.slot_kv, ...), custom_call_target="tpu_custom_call" | custom-call | tf_op jit(solution)/shard_map/attend_backward/pallas_call | solution.py:390
  210.4 4.3 copy.46
  214.6 4.0 copy.49
  220.6 64.6 %reduce-scatter.19.cloned.1.call-done = bf16[48,2304]{1,0:T(8,128)(2,1)} async-done(((bf16[768,2304]{1,0:T(8,128)(2,1)}), bf16[48,2304]{1,0:T(8,128)(2,1)}) %reduce-scatter.19.cloned.1.call-update) | async-done | bytes 221200
  285.2 2.0 copy.50
  287.1 58.6 %reduce-scatter.13.cloned.1.call-done = bf16[48,768]{1,0:T(8,128)(2,1)} async-done(((bf16[768,768]{1,0:T(8,128)(2,1)}), bf16[48,768]{1,0:T(8,128)(2,1)}) %reduce-scatter.13.cloned.1.call-update) | async-done | bytes 73744 | tf_op jit(solution)/shard_map/reduce_scatter | solution.py:427
  345.7 78.4 %reduce-scatter.15.cloned.1.call-done = bf16[48,3072]{1,0:T(8,128)(2,1)} async-done(((bf16[768,3072]{1,0:T(8,128)(2,1)}), bf16[48,3072]{1,0:T(8,128)(2,1)}) %reduce-scatter.15.cloned.1.call-update) | async-done | bytes 294928 | tf_op jit(solution)/shard_map/reduce_scatter | solution.py:427
  424.1 78.8 %reduce-scatter.17.cloned.1.call-done = bf16[192,768]{1,0:T(8,128)(2,1)} async-done(((bf16[3072,768]{1,0:T(8,128)(2,1)}), bf16[192,768]{1,0:T(8,128)(2,1)}) %reduce-scatter.17.cloned.1.call-update) | async-done | bytes 294928 | tf_op jit(solution)/shard_map/reduce_scatter | solution.py:427
  503.2 11.9 %broadcast_in_dim.54 = f32[128,64,768]{2,1,0:T(8,128)} broadcast(f32[]{:T(128)} %constant.43.clone.1), dimensions={} | broadcast | bytes 25165828 | tf_op jit(solution)/shard_map/broadcast_in_dim | solution.py:410
  515.1 15.8 %scatter_fusion = f32[128,64,768]{2,1,0:T(8,128)} fusion(f32[128,64,768]{2,1,0:T(8,128)} %broadcast_in_dim.54, s32[28]{0:T(128)S(1)} %fusion.17, f32[28,64,768]{2,1,0:T(8,128)} %bitcast.77), kind=kCustom, calls=%fused_computation | custom fusion | flops 1376256 | bytes 16515184 | tf_op jit(solution)/shard_map/scatter-add | solution.py:411
  530.9 13.9 %convert_element_type.35 = bf16[128,64,768]{2,1,0:T(8,128)(2,1)} convert(f32[128,64,768]{2,1,0:T(8,128)} %scatter_fusion) | non-fusion elementwise | flops 6291456 | bytes 37748736 | tf_op jit(solution)/shard_map/convert_element_type | solution.py:413
  544.8 5.2 all-reduce.3.cloned.1.call-done
  550.0 2.0 copy.47
  552.0 1.6 convert_element_type.39
  553.6 1.8 convert_element_type.40
  555.4 1.8 convert_element_type.41
  557.2 131.7 %reduce-scatter.11.cloned.1.call-done = bf16[512,768]{1,0:T(8,128)(2,1)} async-done(((bf16[8192,768]{1,0:T(8,128)(2,1)}), bf16[512,768]{1,0:T(8,128)(2,1)}) %reduce-scatter.11.cloned.1.call-update) | async-done | bytes 786448 | tf_op jit(solution)/shard_map/reduce_scatter | solution.py:412
  689.0 2.1 fusion.13
  692.1 2.9 fusion.16
  695.0 52.2 %reduce-scatter.21.cloned.1.call-done = f32[48,4]{1,0:T(8,128)} async-done(((f32[768,4]{1,0:T(8,128)}), f32[48,4]{1,0:T(8,128)}) %reduce-scatter.21.cloned.1.call-update) | async-done | bytes 784
  748.1 4.9 psum.39
  (65 shorter events, 12.9 us)
Async XLA Ops:
  7.2 17.9 %copy-start = (bf16[1,512,768]{2,1,0:T(8,128)(2,1)S(1)}, bf16[1,512,768]{2,1,0:T(8,128)(2,1)}, u32[]{:S(2)}) copy-start(bf16[1,512,768]{2,1,0:T(8,128)(2,1)} %param.14) | copy-start | bytes 2359300
  7.2 18.3 %copy-start.7 = (f32[768]{0:T(1024)S(1)}, f32[768]{0:T(1024)}, u32[]{:S(2)}) copy-start(f32[768]{0:T(1024)} %param.20) | copy-start | bytes 9220
  7.2 18.3 %copy-start.6 = (f32[768]{0:T(1024)S(1)}, f32[768]{0:T(1024)}, u32[]{:S(2)}) copy-start(f32[768]{0:T(1024)} %param.19) | copy-start | bytes 9220
  7.2 106.6 %all-gather.2.cloned.1.call-start = ((), (), s32[]{:S(2)}) async-start(), calls=%async_computation.6 | async-start | bytes 13369344 | tf_op jit(solution)/shard_map/all_gather | solution.py:325
  7.9 277.2 %reduce-scatter.19.cloned.1.call-start = ((), (), s32[]{:S(2)}) async-start(), calls=%async_computation.11 | async-start | bytes 3760128
  25.8 4.3 copy-start.3
  30.2 2.6 copy-start.5
  218.6 127.1 %reduce-scatter.13.cloned.1.call-start = ((), (), s32[]{:S(2)}) async-start(), calls=%async_computation.8 | async-start | bytes 1253376 | tf_op jit(solution)/shard_map/reduce_scatter | solution.py:427
  219.4 204.7 %reduce-scatter.15.cloned.1.call-start = ((), (), s32[]{:S(2)}) async-start(), calls=%async_computation.9 | async-start | bytes 5013504 | tf_op jit(solution)/shard_map/reduce_scatter | solution.py:427
  219.9 283.0 %reduce-scatter.17.cloned.1.call-start = ((), (), s32[]{:S(2)}) async-start(), calls=%async_computation.10 | async-start | bytes 5013504 | tf_op jit(solution)/shard_map/reduce_scatter | solution.py:427
  220.5 329.5 %all-reduce.3.cloned.1.call-start = ((), (), s32[]{:S(2)}) async-start(), calls=%async_computation.13 | async-start | bytes 2506752 | tf_op jit(solution)/shard_map/psum | solution.py:428
  502.9 186.0 %reduce-scatter.11.cloned.1.call-start = ((), (), s32[]{:S(2)}) async-start(), calls=%async_computation.7 | async-start | bytes 13369344 | tf_op jit(solution)/shard_map/reduce_scatter | solution.py:412
  544.8 144.2 %copy-start.1 = (bf16[1,512,768]{2,1,0:T(8,128)(2,1)S(1)}, bf16[1,512,768]{2,1,0:T(8,128)(2,1)}, u32[]{:S(2)}) copy-start(bf16[1,512,768]{2,1,0:T(8,128)(2,1)} %param.14) | copy-start | bytes 2359300
  544.8 144.2 %copy-start.2 = (f32[512,768]{1,0:T(8,128)S(1)}, f32[512,768]{1,0:T(8,128)}, u32[]{:S(2)}) copy-start(f32[512,768]{1,0:T(8,128)} %get-tuple-element.32) | copy-start | bytes 4718596
  544.8 202.5 %reduce-scatter.21.cloned.1.call-start = ((), (), s32[]{:S(2)}) async-start(), calls=%async_computation.12 | async-start | bytes 417792
  689.0 2.1 copy-start.8
  689.0 2.1 copy-start.9
  689.0 3.1 copy-start.4
Sparse Core Ops, SparseCore 0:
  10.3 103.4 all-gather.1
  218.7 66.3 reduce-scatter.18
  288.8 56.9 reduce-scatter.12
  349.4 74.5 reduce-scatter.14
  428.3 74.5 reduce-scatter.16
  505.8 44.1 all-reduce.2
  554.0 134.8 reduce-scatter.10
  692.5 54.7 reduce-scatter.20
